TPU v7x, 128 devices: a whole 4x4x4 slice. The times are simulated.
128 devices in a mesh: lat: 8 (over y, core), elev: 16 (over z, x).
Axes of the slice: x: 4, y: 4, z: 4, core: 2. Of those that a mesh axis runs over, the one named last changes fastest.
Arguments:
- frames: float32 [512, 512, 2048], P('lat', 'elev')
- start_basis: float32 [512, 96], replicated, may hold values from -6 to 6
Outputs:
- core: float32 [512, 96, 2048], P('lat', None, 'elev')
- basis: float32 [512, 96], P('elev')
All inputs are finite; a program needn't handle non-finite values.
Results may differ from a plain program's by a relative error of at most 0.00024.
Values sent between devices are 32-bit elements; how exact they have to be, the bound alone decides.
A program may use at most 192 MiB of HBM per device.

v0:
```python
import functools

import jax
import jax.numpy as jnp
from jax import lax
from jax.experimental import pallas as pl
from jax.experimental.pallas import tpu as pltpu
from jax.sharding import PartitionSpec as P

ITERS = 3
HIGHEST = lax.Precision.HIGHEST
LANES = 128
STEP = 2
CORE_STEP = 16
Z = 4
X = 4
PARTS = ((0, 24), (24, 16))


def dot_nt(a, b):
    return lax.dot_general(
        a, b, (((1,), (1,)), ((), ())), precision=HIGHEST, preferred_element_type=jnp.float32
    )


def hops(offset):
    return min(offset[0], Z - offset[0]) + min(offset[1], X - offset[1])


def gather_gram_kernel(
    frames, x_out, g_out, buf, gacc, packed, half_in, half, ring_in, part, y_in, total, half_all,
    recv, send, ar_recv, ar_send, out_sem,
):
    lines = frames.shape[0]
    own = frames.shape[1]
    chunks = lines // STEP
    lat = lax.axis_index("lat")
    elev = lax.axis_index("elev")
    core = lax.rem(lat, 2)
    y = lat // 2
    x = lax.rem(elev, X)
    z = elev // X
    partner = lat + 1 - 2 * core
    offsets = sorted([(dz, dx) for dz in range(Z) for dx in range(X) if dz or dx], key=hops)
    far_first = [lax.rem(z + dz, Z) * X + lax.rem(x + dx, X) for dz, dx in reversed(offsets)]
    peers = []
    for n in range(len(far_first)):
        peers.append(far_first[n // 2] if n % 2 else far_first[len(far_first) - 1 - n // 2])
    y_peers = [lax.rem(y + dy, 4) * 2 + core for dy in (2, 1, 3)]

    barrier = pltpu.get_barrier_semaphore()
    for p in peers:
        pl.semaphore_signal(barrier, inc=1, device_id={"elev": p}, device_id_type=pl.DeviceIdType.MESH)
    for q in y_peers + [partner]:
        pl.semaphore_signal(barrier, inc=1, device_id={"lat": q}, device_id_type=pl.DeviceIdType.MESH)
    pl.semaphore_wait(barrier, len(peers) + len(y_peers) + 1)

    gacc[...] = jnp.zeros_like(gacc)
    mine = pl.ds(pl.multiple_of(elev * own, own), own)

    def issue(c, _):
        rows = pl.ds(c * STEP, STEP)
        for p in peers:
            pltpu.make_async_remote_copy(
                src_ref=frames.at[rows, :, pl.ds(pl.multiple_of(p * LANES, LANES), LANES)],
                dst_ref=buf.at[rows, mine, :],
                send_sem=send.at[c],
                recv_sem=recv.at[c],
                device_id={"elev": p},
                device_id_type=pl.DeviceIdType.MESH,
            ).start()
        pltpu.make_async_copy(
            frames.at[rows, :, pl.ds(pl.multiple_of(elev * LANES, LANES), LANES)],
            buf.at[rows, mine, :],
            recv.at[c],
        ).start()
        return 0

    lax.fori_loop(0, chunks, issue, 0)

    def consume(c, _):
        rows = pl.ds(c * STEP, STEP)
        pltpu.make_async_copy(buf.at[rows], buf.at[rows], recv.at[c]).wait()
        pltpu.make_async_copy(buf.at[rows], x_out.at[rows], out_sem.at[c]).start()
        block = jnp.concatenate([buf[c * STEP + i] for i in range(STEP)], axis=1)
        low, high = block[:256], block[256:]
        gacc[0] += dot_nt(low, low)
        gacc[1] += dot_nt(high, low)
        gacc[2] += dot_nt(high, high)
        return 0

    lax.fori_loop(0, chunks, consume, 0)

    places = [(0, 0, 0), (0, 1, 0), (0, 1, 1), (1, 0, 0), (1, 0, 1), (1, 1, 0), (1, 1, 1), (2, 0, 0), (2, 1, 0), (2, 1, 1)]
    blocks = [gacc[g, pl.ds(i * 128, 128), pl.ds(j * 128, 128)] for g, i, j in places]
    packed[...] = jnp.concatenate(blocks, axis=0).reshape(packed.shape)

    plane = Z * X
    parts = [(k, pl.ds(first, count)) for k, (first, count) in enumerate(PARTS)]
    kept = pl.ds(core * plane, plane)
    given = pl.ds((1 - core) * plane, plane)

    def to_partner(src, dst, hop, k):
        return pltpu.make_async_remote_copy(
            src_ref=src,
            dst_ref=dst,
            send_sem=ar_send.at[hop, k],
            recv_sem=ar_recv.at[hop, k],
            device_id={"lat": partner},
            device_id_type=pl.DeviceIdType.MESH,
        )

    def send_all(src_of, dst, axis, targets, hop, k, mine_src):
        for p in targets:
            pltpu.make_async_remote_copy(
                src_ref=src_of(p),
                dst_ref=dst,
                send_sem=ar_send.at[hop, k],
                recv_sem=ar_recv.at[hop, k],
                device_id={axis: p},
                device_id_type=pl.DeviceIdType.MESH,
            ).start()
        pltpu.make_async_copy(mine_src, dst, ar_recv.at[hop, k]).start()

    swaps = [to_partner(packed.at[given, rows], half_in.at[:, rows], 0, k) for k, rows in parts]
    for swap in swaps:
        swap.start()
    for k, rows in parts:
        swaps[k].wait()
        half[:, rows] = packed[kept, rows] + half_in[:, rows]
        send_all(lambda p: half.at[p, rows], ring_in.at[elev, rows], "elev", far_first, 1, k, half.at[elev, rows])
    for k, rows in parts:
        pltpu.make_async_copy(ring_in.at[:, rows], ring_in.at[:, rows], ar_recv.at[1, k]).wait()
        part[rows] = jnp.sum(ring_in[:, rows], axis=0)
        send_all(lambda q: part.at[rows], y_in.at[y, rows], "lat", y_peers, 2, k, part.at[rows])
    for k, rows in parts:
        pltpu.make_async_copy(y_in.at[:, rows], y_in.at[:, rows], ar_recv.at[2, k]).wait()
        total[rows] = (y_in[0, rows] + y_in[1, rows]) + (y_in[2, rows] + y_in[3, rows])
        send_all(lambda p: total.at[rows], half_all.at[elev, rows], "elev", far_first, 3, k, total.at[rows])
    swaps = [to_partner(half_all.at[:, rows], g_out.at[kept, rows], 4, k) for k, rows in parts]
    for k, rows in parts:
        pltpu.make_async_copy(half_all.at[:, rows], half_all.at[:, rows], ar_recv.at[3, k]).wait()
        swaps[k].start()
        g_out[kept, rows] = half_all[:, rows]
    for swap in swaps:
        swap.wait()

    n = plane - 1
    for k, rows in parts:
        for hop, gone in ((1, half.at[pl.ds(0, n), rows]), (2, y_in.at[pl.ds(0, 3), rows]), (3, half.at[pl.ds(0, n), rows])):
            pltpu.make_async_copy(gone, gone, ar_send.at[hop, k]).wait()

    def drain(c, _):
        rows = pl.ds(c * STEP, STEP)
        gone = buf.at[rows, pl.ds(0, n * own), :]
        pltpu.make_async_copy(gone, gone, send.at[c]).wait()
        pltpu.make_async_copy(buf.at[rows], x_out.at[rows], out_sem.at[c]).wait()
        return 0

    lax.fori_loop(0, chunks, drain, 0)


def gather_gram(frames):
    lines, own, columns = frames.shape
    elevs = own * Z * X
    chunks = lines // STEP
    plane = Z * X
    shard = 1280 // (2 * plane)
    return pl.pallas_call(
        gather_gram_kernel,
        out_shape=(
            jax.ShapeDtypeStruct((lines, elevs, LANES), jnp.float32),
            jax.ShapeDtypeStruct((2 * plane, shard, LANES), jnp.float32),
        ),
        in_specs=[pl.BlockSpec(memory_space=pl.ANY)],
        out_specs=(pl.BlockSpec(memory_space=pl.ANY), pl.BlockSpec(memory_space=pltpu.VMEM)),
        scratch_shapes=[
            pltpu.VMEM((lines, elevs, LANES), jnp.float32),
            pltpu.VMEM((3, 256, 256), jnp.float32),
            pltpu.VMEM((2 * plane, shard, LANES), jnp.float32),
            pltpu.VMEM((plane, shard, LANES), jnp.float32),
            pltpu.VMEM((plane, shard, LANES), jnp.float32),
            pltpu.VMEM((plane, shard, LANES), jnp.float32),
            pltpu.VMEM((shard, LANES), jnp.float32),
            pltpu.VMEM((4, shard, LANES), jnp.float32),
            pltpu.VMEM((shard, LANES), jnp.float32),
            pltpu.VMEM((plane, shard, LANES), jnp.float32),
            pltpu.SemaphoreType.DMA((chunks,)),
            pltpu.SemaphoreType.DMA((chunks,)),
            pltpu.SemaphoreType.DMA((5, len(PARTS))),
            pltpu.SemaphoreType.DMA((5, len(PARTS))),
            pltpu.SemaphoreType.DMA((chunks,)),
        ],
        compiler_params=pltpu.CompilerParams(
            collective_id=0, has_side_effects=True, vmem_limit_bytes=48 * 1024 * 1024
        ),
        cost_estimate=pl.CostEstimate(
            flops=2 * lines * LANES * elevs * elevs, bytes_accessed=3 * frames.size * 4, transcendentals=0
        ),
        name="gather_gram",
    )(frames)


def iota(shape, dim):
    return lax.broadcasted_iota(jnp.int32, shape, dim)


def dot_nn(a, b):
    return jnp.dot(a, b, precision=HIGHEST, preferred_element_type=jnp.float32)


def split(v):
    high = v.astype(jnp.bfloat16)
    return high, (v - high.astype(jnp.float32)).astype(jnp.bfloat16)


def cholesky_inverse(m):
    n = m.shape[0]
    tiles = n // 8
    sub, lane = iota((8, n), 0), iota((8, n), 1)

    def up(row):
        return jnp.broadcast_to(row, (8, n))

    def along(tile, j):
        return jnp.broadcast_to(tile[:, j : j + 1], (8, n))

    a = [m[8 * i : 8 * i + 8, :] for i in range(tiles)]
    out = []
    diagonal = [along(a[0], t) for t in range(8)]
    for p in range(tiles):
        j = 8 * p
        columns = [[along(a[i], j + t) for i in range(p + 1, tiles)] for t in range(8)]
        ahead = [along(a[p + 1], j + 8 + s) for s in range(8)] if p + 1 < tiles else []
        panel = (lane >= j) & (lane < j + 8)
        row = jnp.where(panel, jnp.where(lane == sub + j, 1.0, 0.0), a[p])
        below = [jnp.where(panel, 0.0, a[i]) for i in range(p + 1, tiles)]
        pivots = diagonal[0]
        for t in range(8):
            pivot = up(diagonal[t][t : t + 1, :])
            inverse = 1.0 / pivot
            if t:
                pivots = jnp.where(sub == t, pivot, pivots)
            g = jnp.where(sub > t, diagonal[t] * inverse, 0.0)
            f = [q * inverse for q in columns[t]]
            for s in range(t + 1, 8):
                scale = up(diagonal[t][s : s + 1, :])
                diagonal[s] = diagonal[s] - g * scale
                columns[s] = [q - h * scale for q, h in zip(columns[s], f)]
            ahead = [q - f[0] * up(columns[t][0][s : s + 1, :]) for s, q in enumerate(ahead)]
            pivot_row = up(row[t : t + 1, :])
            row = row - g * pivot_row
            below = [q - h * pivot_row for q, h in zip(below, f)]
        a = a[: p + 1] + below
        diagonal = ahead
        out.append(jnp.where(lane < j + 8, row, 0.0) * lax.rsqrt(pivots))
    return jnp.concatenate(out, axis=0)


def orth_again(w, result):
    m = dot_nt(w, w)
    row, column = iota(m.shape, 0), iota(m.shape, 1)
    e = m - jnp.where(row == column, 1.0, 0.0)
    lower = jnp.where(row > column, e, jnp.where(row == column, 0.5 * e, 0.0))
    result[...] = w - jnp.dot(lower.astype(jnp.bfloat16), w.astype(jnp.bfloat16), preferred_element_type=jnp.float32)

    @pl.when(jnp.logical_not(jnp.sum(e * e) <= 3e-8))
    def _():
        result[...] = dot_nn(cholesky_inverse(m), w)


def basis_core_kernel(x, packed, start, core, basis_out, buf, first, gram, out, turned, in_sem, start_sem, out_sem):
    chunks = x.shape[0] // CORE_STEP

    def load(c):
        rows = pl.ds(c * CORE_STEP, CORE_STEP)
        return pltpu.make_async_copy(x.at[rows], buf.at[rows], in_sem.at[c])

    def store(c):
        rows = pl.ds(c * CORE_STEP, CORE_STEP)
        return pltpu.make_async_copy(out.at[rows], core.at[rows], out_sem.at[c])

    begin = pltpu.make_async_copy(start, first, start_sem)
    begin.start()
    for c in range(chunks):
        load(c).start()

    places = [(0, 0), (1, 0), (1, 1), (2, 0), (2, 1), (3, 0), (3, 1), (2, 2), (3, 2), (3, 3)]
    for n, (i, j) in enumerate(places):
        tile = packed[pl.ds(n * 128, 128), :]
        gram[pl.ds(i * 128, 128), pl.ds(j * 128, 128)] = tile
        if i != j:
            gram[pl.ds(j * 128, 128), pl.ds(i * 128, 128)] = tile.T

    def turn(_, carry):
        w = dot_nn(first[...], gram[...])
        w = dot_nn(cholesky_inverse(dot_nt(w, w)), w)
        orth_again(w, first)
        return carry

    begin.wait()
    lax.fori_loop(0, ITERS, turn, 0)
    basis = first[...]
    turned[...] = basis.T
    own = basis_out.shape[0]
    basis_out[...] = turned[pl.ds(pl.multiple_of(lax.axis_index("elev") * own, 8), own), :]

    high, low = split(basis)
    both = jnp.concatenate([high, low], axis=0)
    kept = basis.shape[0]

    for c in range(chunks):
        load(c).wait()

    def project(c, _):
        for i in range(0, CORE_STEP, 2):
            l = c * CORE_STEP + i
            xh, xl = split(jnp.concatenate([buf[l], buf[l + 1]], axis=1))
            r = jnp.dot(both, xh, preferred_element_type=jnp.float32)
            q = jnp.dot(high, xl, preferred_element_type=jnp.float32)
            s = r[:kept] + (r[kept:] + q)
            out[l] = s[:, :LANES]
            out[l + 1] = s[:, LANES:]
        store(c).start()
        return 0

    lax.fori_loop(0, chunks, project, 0)

    def drain(c, _):
        store(c).wait()
        return 0

    lax.fori_loop(0, chunks, drain, 0)


def basis_core(x, packed, start, own):
    lines, elevs, lanes = x.shape
    kept = start.shape[0]
    chunks = lines // CORE_STEP
    return pl.pallas_call(
        basis_core_kernel,
        out_shape=(
            jax.ShapeDtypeStruct((lines, kept, lanes), jnp.float32),
            jax.ShapeDtypeStruct((own, kept), jnp.float32),
        ),
        in_specs=[pl.BlockSpec(memory_space=p) for p in (pl.ANY, pltpu.VMEM, pl.ANY)],
        out_specs=(pl.BlockSpec(memory_space=pl.ANY), pl.BlockSpec(memory_space=pltpu.VMEM)),
        scratch_shapes=[
            pltpu.VMEM((lines, elevs, lanes), jnp.float32),
            pltpu.VMEM((kept, elevs), jnp.float32),
            pltpu.VMEM((elevs, elevs), jnp.float32),
            pltpu.VMEM((lines, kept, lanes), jnp.float32),
            pltpu.VMEM((elevs, kept), jnp.float32),
            pltpu.SemaphoreType.DMA((chunks,)),
            pltpu.SemaphoreType.DMA,
            pltpu.SemaphoreType.DMA((chunks,)),
        ],
        compiler_params=pltpu.CompilerParams(vmem_limit_bytes=48 * 1024 * 1024),
        cost_estimate=pl.CostEstimate(
            flops=6 * lines * lanes * elevs * kept, bytes_accessed=2 * x.size * 4, transcendentals=0
        ),
        name="basis_core",
    )(x, packed, start)


def per_device(frames, start_basis):
    regrouped, packed = gather_gram(frames)
    return basis_core(regrouped, packed.reshape(-1, LANES), start_basis.T, frames.shape[1])


def solution(mesh):
    return jax.shard_map(
        per_device,
        mesh=mesh,
        in_specs=(P("lat", "elev", None), P()),
        out_specs=(P("lat", None, "elev"), P("elev", None)),
        check_vma=False,
    )
```

profile of v0, /device:TPU:1, one launch (start us, length us, event | category | flops | bytes accessed | tf_op | source)
XLA Modules:
  0.0 230.1 jit_solution(1899595358722639665)
XLA Ops:
  0.6 0.0 copy-start
  0.6 212.3 %gather_gram.1 = (f32[64,512,128]{2,1,0:T(8,128)}, f32[32,40,128]{2,1,0:T(8,128)S(1)}) custom-call(f32[64,32,2048]{2,1,0:T(8,128)} %frames.1), custom_call_target="tpu_custom_call" | custom-call | flops 4294967296 | bytes 50331648 | tf_op jit(solution)/shard_map/gather_gram/pallas_call | solution.py:169
  213.0 0.0 copy-done
  213.0 17.2 %basis_core.1 = (f32[64,96,128]{2,1,0:T(8,128)}, f32[32,96]{1,0:T(8,128)}) custom-call(f32[64,512,128]{2,1,0:T(8,128)} %get-tuple-element.4.x, f32[1280,128]{1,0:T(8,128)S(1)} %bitcast.2, f32[96,512]{1,0:T(8,128)S(1)} %bitcast.3), custom_call_target="tpu_custom_call" | custom-call | flops 2415919104 | bytes 33554432 | tf_op jit(solution)/shard_map/basis_core/pallas_call | solution.py:340
Async XLA Ops:
  0.6 212.3 %copy-start = (f32[512,96]{0,1:T(8,128)S(1)}, f32[512,96]{0,1:T(8,128)}, u32[]{:S(2)}) copy-start(f32[512,96]{0,1:T(8,128)} %param.3) | copy-start | bytes 589828
where the time goes:
time: 230 us
  Pallas kernels  229 us (100%)
    pallas_call x1, Pallas kernels, gather_gram(): pl.pallas_call(gather_gram_kernel, out_shape=(jax.ShapeDtypeStruct((lines...  212 us
    pallas_call x1, Pallas kernels, basis_core(): pl.pallas_call(basis_core_kernel, out_shape=(jax.ShapeDtypeStruct((lines,...  17.2 us

commit v1 on v0

--- a/solution.py
+++ b/solution.py
@@ -10,7 +10,7 @@
 ITERS = 3
 HIGHEST = lax.Precision.HIGHEST
 LANES = 128
-STEP = 2
+STEP = 4
 CORE_STEP = 16
 Z = 4
 X = 4
@@ -129,6 +129,15 @@
         swaps[k].wait()
         half[:, rows] = packed[kept, rows] + half_in[:, rows]
         send_all(lambda p: half.at[p, rows], ring_in.at[elev, rows], "elev", far_first, 1, k, half.at[elev, rows])
+    def drain(c, _):
+        rows = pl.ds(c * STEP, STEP)
+        gone = buf.at[rows, pl.ds(0, (plane - 1) * own), :]
+        pltpu.make_async_copy(gone, gone, send.at[c]).wait()
+        pltpu.make_async_copy(buf.at[rows], x_out.at[rows], out_sem.at[c]).wait()
+        return 0
+
+    lax.fori_loop(0, chunks, drain, 0)
+
     for k, rows in parts:
         pltpu.make_async_copy(ring_in.at[:, rows], ring_in.at[:, rows], ar_recv.at[1, k]).wait()
         part[rows] = jnp.sum(ring_in[:, rows], axis=0)
@@ -149,15 +158,6 @@
     for k, rows in parts:
         for hop, gone in ((1, half.at[pl.ds(0, n), rows]), (2, y_in.at[pl.ds(0, 3), rows]), (3, half.at[pl.ds(0, n), rows])):
             pltpu.make_async_copy(gone, gone, ar_send.at[hop, k]).wait()
-
-    def drain(c, _):
-        rows = pl.ds(c * STEP, STEP)
-        gone = buf.at[rows, pl.ds(0, n * own), :]
-        pltpu.make_async_copy(gone, gone, send.at[c]).wait()
-        pltpu.make_async_copy(buf.at[rows], x_out.at[rows], out_sem.at[c]).wait()
-        return 0
-
-    lax.fori_loop(0, chunks, drain, 0)
 
 
 def gather_gram(frames):
@@ -257,19 +257,30 @@
     return jnp.concatenate(out, axis=0)
 
 
-def orth_again(w, result):
-    m = dot_nt(w, w)
+def split3(v):
+    high = v.astype(jnp.bfloat16)
+    rest = v - high.astype(jnp.float32)
+    middle = rest.astype(jnp.bfloat16)
+    return high, middle, (rest - middle.astype(jnp.float32)).astype(jnp.bfloat16)
+
+
+def dot_parts(a, b):
+    rows = a.shape[0]
+    a = split3(a)
+    first = jnp.dot(jnp.concatenate(a, axis=0), b[0][...], preferred_element_type=jnp.float32)
+    second = jnp.dot(jnp.concatenate(a[:2], axis=0), b[1][...], preferred_element_type=jnp.float32)
+    third = jnp.dot(a[0], b[2][...], preferred_element_type=jnp.float32)
+    return first[:rows] + (first[rows : 2 * rows] + second[:rows] + (first[2 * rows :] + second[rows:] + third))
+
+
+def near_identity(m):
     row, column = iota(m.shape, 0), iota(m.shape, 1)
     e = m - jnp.where(row == column, 1.0, 0.0)
     lower = jnp.where(row > column, e, jnp.where(row == column, 0.5 * e, 0.0))
-    result[...] = w - jnp.dot(lower.astype(jnp.bfloat16), w.astype(jnp.bfloat16), preferred_element_type=jnp.float32)
-
-    @pl.when(jnp.logical_not(jnp.sum(e * e) <= 3e-8))
-    def _():
-        result[...] = dot_nn(cholesky_inverse(m), w)
-
-
-def basis_core_kernel(x, packed, start, core, basis_out, buf, first, gram, out, turned, in_sem, start_sem, out_sem):
+    return jnp.sum(e * e) <= 3e-8, lower.astype(jnp.bfloat16)
+
+
+def basis_core_kernel(x, packed, start, core, basis_out, buf, first, gram, out, turned, wide, gh, gm, gl, in_sem, start_sem, out_sem):
     chunks = x.shape[0] // CORE_STEP
 
     def load(c):
@@ -292,14 +303,38 @@
         if i != j:
             gram[pl.ds(j * 128, 128), pl.ds(i * 128, 128)] = tile.T
 
-    def turn(_, carry):
-        w = dot_nn(first[...], gram[...])
+    for part, value in zip((gh, gm, gl), split3(gram[...])):
+        part[...] = value
+
+    begin.wait()
+    wide[...] = dot_parts(first[...], (gh, gm, gl))
+
+    def turn(last):
+        w = wide[...]
         w = dot_nn(cholesky_inverse(dot_nt(w, w)), w)
-        orth_again(w, first)
+        m = dot_nt(w, w)
+        near, lower = near_identity(m)
+
+        def corrected(v):
+            return v - jnp.dot(lower, v.astype(jnp.bfloat16), preferred_element_type=jnp.float32)
+
+        if last:
+            first[...] = corrected(w)
+        else:
+            wide[...] = corrected(dot_parts(w, (gh, gm, gl)))
+
+        @pl.when(jnp.logical_not(near))
+        def _():
+            first[...] = dot_nn(cholesky_inverse(m), w)
+            if not last:
+                wide[...] = dot_parts(first[...], (gh, gm, gl))
+
+    def earlier_turn(_, carry):
+        turn(False)
         return carry
 
-    begin.wait()
-    lax.fori_loop(0, ITERS, turn, 0)
+    lax.fori_loop(0, ITERS - 1, earlier_turn, 0)
+    turn(True)
     basis = first[...]
     turned[...] = basis.T
     own = basis_out.shape[0]
@@ -351,6 +386,10 @@
             pltpu.VMEM((elevs, elevs), jnp.float32),
             pltpu.VMEM((lines, kept, lanes), jnp.float32),
             pltpu.VMEM((elevs, kept), jnp.float32),
+            pltpu.VMEM((kept, elevs), jnp.float32),
+            pltpu.VMEM((elevs, elevs), jnp.bfloat16),
+            pltpu.VMEM((elevs, elevs), jnp.bfloat16),
+            pltpu.VMEM((elevs, elevs), jnp.bfloat16),
             pltpu.SemaphoreType.DMA((chunks,)),
             pltpu.SemaphoreType.DMA,
             pltpu.SemaphoreType.DMA((chunks,)),

time: 230 us -> 229 us (level)
  no operation moved by 1% of the time
where the time goes in v1:
time: 229 us
  Pallas kernels  228 us (100%)
    pallas_call x1, Pallas kernels, gather_gram(): pl.pallas_call(gather_gram_kernel, out_shape=(jax.ShapeDtypeStruct((lines...  211 us
    pallas_call x1, Pallas kernels, basis_core(): pl.pallas_call(basis_core_kernel, out_shape=(jax.ShapeDtypeStruct((lines,...  16.5 us

profile of v1, /device:TPU:1, one launch (start us, length us, event | category | flops | bytes accessed | tf_op | source)
XLA Modules:
  0.0 228.6 jit_solution(14162167258482927073)
XLA Ops:
  0.6 0.0 copy-start
  0.6 211.3 %gather_gram.1 = (f32[64,512,128]{2,1,0:T(8,128)}, f32[32,40,128]{2,1,0:T(8,128)S(1)}) custom-call(f32[64,32,2048]{2,1,0:T(8,128)} %frames.1), custom_call_target="tpu_custom_call" | custom-call | flops 4294967296 | bytes 50331648 | tf_op jit(solution)/shard_map/gather_gram/pallas_call | solution.py:169
  211.9 0.0 copy-done
  211.9 16.5 %basis_core.1 = (f32[64,96,128]{2,1,0:T(8,128)}, f32[32,96]{1,0:T(8,128)}) custom-call(f32[64,512,128]{2,1,0:T(8,128)} %get-tuple-element.4.x, f32[1280,128]{1,0:T(8,128)S(1)} %bitcast.2, f32[96,512]{1,0:T(8,128)S(1)} %bitcast.3), custom_call_target="tpu_custom_call" | custom-call | flops 2415919104 | bytes 33554432 | tf_op jit(solution)/shard_map/basis_core/pallas_call | solution.py:375
Async XLA Ops:
  0.6 211.3 %copy-start = (f32[512,96]{0,1:T(8,128)S(1)}, f32[512,96]{0,1:T(8,128)}, u32[]{:S(2)}) copy-start(f32[512,96]{0,1:T(8,128)} %param.3) | copy-start | bytes 589828

commit v2 on v1

--- a/solution.py
+++ b/solution.py
@@ -11,6 +11,7 @@
 HIGHEST = lax.Precision.HIGHEST
 LANES = 128
 STEP = 4
+LAST = (2, 1, 1)
 CORE_STEP = 16
 Z = 4
 X = 4
@@ -33,7 +34,8 @@
 ):
     lines = frames.shape[0]
     own = frames.shape[1]
-    chunks = lines // STEP
+    chunks = (lines - sum(LAST)) // STEP
+    tail = [(chunks + n, lines - sum(LAST[n:]), count) for n, count in enumerate(LAST)]
     lat = lax.axis_index("lat")
     elev = lax.axis_index("elev")
     core = lax.rem(lat, 2)
@@ -58,8 +60,8 @@
     gacc[...] = jnp.zeros_like(gacc)
     mine = pl.ds(pl.multiple_of(elev * own, own), own)
 
-    def issue(c, _):
-        rows = pl.ds(c * STEP, STEP)
+    def issue(c, first, count):
+        rows = pl.ds(first, count)
         for p in peers:
             pltpu.make_async_remote_copy(
                 src_ref=frames.at[rows, :, pl.ds(pl.multiple_of(p * LANES, LANES), LANES)],
@@ -76,20 +78,24 @@
         ).start()
         return 0
 
-    lax.fori_loop(0, chunks, issue, 0)
-
-    def consume(c, _):
-        rows = pl.ds(c * STEP, STEP)
+    lax.fori_loop(0, chunks, lambda c, _: issue(c, c * STEP, STEP), 0)
+    for c, first, count in tail:
+        issue(c, first, count)
+
+    def consume(c, first, count):
+        rows = pl.ds(first, count)
         pltpu.make_async_copy(buf.at[rows], buf.at[rows], recv.at[c]).wait()
         pltpu.make_async_copy(buf.at[rows], x_out.at[rows], out_sem.at[c]).start()
-        block = jnp.concatenate([buf[c * STEP + i] for i in range(STEP)], axis=1)
+        block = jnp.concatenate([buf[first + i] for i in range(count)], axis=1)
         low, high = block[:256], block[256:]
         gacc[0] += dot_nt(low, low)
         gacc[1] += dot_nt(high, low)
         gacc[2] += dot_nt(high, high)
         return 0
 
-    lax.fori_loop(0, chunks, consume, 0)
+    lax.fori_loop(0, chunks, lambda c, _: consume(c, c * STEP, STEP), 0)
+    for c, first, count in tail:
+        consume(c, first, count)
 
     places = [(0, 0, 0), (0, 1, 0), (0, 1, 1), (1, 0, 0), (1, 0, 1), (1, 1, 0), (1, 1, 1), (2, 0, 0), (2, 1, 0), (2, 1, 1)]
     blocks = [gacc[g, pl.ds(i * 128, 128), pl.ds(j * 128, 128)] for g, i, j in places]
@@ -129,14 +135,16 @@
         swaps[k].wait()
         half[:, rows] = packed[kept, rows] + half_in[:, rows]
         send_all(lambda p: half.at[p, rows], ring_in.at[elev, rows], "elev", far_first, 1, k, half.at[elev, rows])
-    def drain(c, _):
-        rows = pl.ds(c * STEP, STEP)
+    def drain(c, first, count):
+        rows = pl.ds(first, count)
         gone = buf.at[rows, pl.ds(0, (plane - 1) * own), :]
         pltpu.make_async_copy(gone, gone, send.at[c]).wait()
         pltpu.make_async_copy(buf.at[rows], x_out.at[rows], out_sem.at[c]).wait()
         return 0
 
-    lax.fori_loop(0, chunks, drain, 0)
+    lax.fori_loop(0, chunks, lambda c, _: drain(c, c * STEP, STEP), 0)
+    for c, first, count in tail:
+        drain(c, first, count)
 
     for k, rows in parts:
         pltpu.make_async_copy(ring_in.at[:, rows], ring_in.at[:, rows], ar_recv.at[1, k]).wait()
@@ -163,7 +171,7 @@
 def gather_gram(frames):
     lines, own, columns = frames.shape
     elevs = own * Z * X
-    chunks = lines // STEP
+    chunks = (lines - sum(LAST)) // STEP + len(LAST)
     plane = Z * X
     shard = 1280 // (2 * plane)
     return pl.pallas_call(
@@ -280,7 +288,7 @@
     return jnp.sum(e * e) <= 3e-8, lower.astype(jnp.bfloat16)
 
 
-def basis_core_kernel(x, packed, start, core, basis_out, buf, first, gram, out, turned, wide, gh, gm, gl, in_sem, start_sem, out_sem):
+def basis_core_kernel(x, packed, start, core, basis_out, buf, first, out, turned, wide, gh, gm, gl, in_sem, start_sem, out_sem):
     chunks = x.shape[0] // CORE_STEP
 
     def load(c):
@@ -299,12 +307,11 @@
     places = [(0, 0), (1, 0), (1, 1), (2, 0), (2, 1), (3, 0), (3, 1), (2, 2), (3, 2), (3, 3)]
     for n, (i, j) in enumerate(places):
         tile = packed[pl.ds(n * 128, 128), :]
-        gram[pl.ds(i * 128, 128), pl.ds(j * 128, 128)] = tile
+        for part, value in zip((gh, gm, gl), split3(tile)):
+            part[pl.ds(i * 128, 128), pl.ds(j * 128, 128)] = value
         if i != j:
-            gram[pl.ds(j * 128, 128), pl.ds(i * 128, 128)] = tile.T
-
-    for part, value in zip((gh, gm, gl), split3(gram[...])):
-        part[...] = value
+            for part, value in zip((gh, gm, gl), split3(tile.T)):
+                part[pl.ds(j * 128, 128), pl.ds(i * 128, 128)] = value
 
     begin.wait()
     wide[...] = dot_parts(first[...], (gh, gm, gl))
@@ -336,10 +343,6 @@
     lax.fori_loop(0, ITERS - 1, earlier_turn, 0)
     turn(True)
     basis = first[...]
-    turned[...] = basis.T
-    own = basis_out.shape[0]
-    basis_out[...] = turned[pl.ds(pl.multiple_of(lax.axis_index("elev") * own, 8), own), :]
-
     high, low = split(basis)
     both = jnp.concatenate([high, low], axis=0)
     kept = basis.shape[0]
@@ -360,6 +363,10 @@
         return 0
 
     lax.fori_loop(0, chunks, project, 0)
+
+    turned[...] = basis.T
+    own = basis_out.shape[0]
+    basis_out[...] = turned[pl.ds(pl.multiple_of(lax.axis_index("elev") * own, 8), own), :]
 
     def drain(c, _):
         store(c).wait()
@@ -383,7 +390,6 @@
         scratch_shapes=[
             pltpu.VMEM((lines, elevs, lanes), jnp.float32),
             pltpu.VMEM((kept, elevs), jnp.float32),
-            pltpu.VMEM((elevs, elevs), jnp.float32),
             pltpu.VMEM((lines, kept, lanes), jnp.float32),
             pltpu.VMEM((elevs, kept), jnp.float32),
             pltpu.VMEM((kept, elevs), jnp.float32),

time: 229 us -> 228 us (level)
  no operation moved by 1% of the time
where the time goes in v2:
time: 228 us
  Pallas kernels  227 us (100%)
    pallas_call x1, Pallas kernels, gather_gram(): pl.pallas_call(gather_gram_kernel, out_shape=(jax.ShapeDtypeStruct((lines...  211 us
    pallas_call x1, Pallas kernels, basis_core(): pl.pallas_call(basis_core_kernel, out_shape=(jax.ShapeDtypeStruct((lines,...  16.5 us

profile of v2, /device:TPU:1, one launch (start us, length us, event | category | flops | bytes accessed | tf_op | source)
XLA Modules:
  0.0 228.2 jit_solution(14798291725903709777)
XLA Ops:
  0.6 0.0 copy-start
  0.6 210.8 %gather_gram.1 = (f32[64,512,128]{2,1,0:T(8,128)}, f32[32,40,128]{2,1,0:T(8,128)S(1)}) custom-call(f32[64,32,2048]{2,1,0:T(8,128)} %frames.1), custom_call_target="tpu_custom_call" | custom-call | flops 4294967296 | bytes 50331648 | tf_op jit(solution)/shard_map/gather_gram/pallas_call | solution.py:177
  211.5 0.0 copy-done
  211.5 16.5 %basis_core.1 = (f32[64,96,128]{2,1,0:T(8,128)}, f32[32,96]{1,0:T(8,128)}) custom-call(f32[64,512,128]{2,1,0:T(8,128)} %get-tuple-element.4.x, f32[1280,128]{1,0:T(8,128)S(1)} %bitcast.2, f32[96,512]{1,0:T(8,128)S(1)} %bitcast.3), custom_call_target="tpu_custom_call" | custom-call | flops 2415919104 | bytes 33554432 | tf_op jit(solution)/shard_map/basis_core/pallas_call | solution.py:382
Async XLA Ops:
  0.6 210.9 %copy-start = (f32[512,96]{0,1:T(8,128)S(1)}, f32[512,96]{0,1:T(8,128)}, u32[]{:S(2)}) copy-start(f32[512,96]{0,1:T(8,128)} %param.3) | copy-start | bytes 589828

commit v3 on v1

--- a/solution.py
+++ b/solution.py
@@ -12,6 +12,7 @@
 LANES = 128
 STEP = 4
 CORE_STEP = 16
+STORE = 4
 Z = 4
 X = 4
 PARTS = ((0, 24), (24, 16))
@@ -288,7 +289,7 @@
         return pltpu.make_async_copy(x.at[rows], buf.at[rows], in_sem.at[c])
 
     def store(c):
-        rows = pl.ds(c * CORE_STEP, CORE_STEP)
+        rows = pl.ds(c * STORE, STORE)
         return pltpu.make_async_copy(out.at[rows], core.at[rows], out_sem.at[c])
 
     begin = pltpu.make_async_copy(start, first, start_sem)
@@ -356,7 +357,8 @@
             s = r[:kept] + (r[kept:] + q)
             out[l] = s[:, :LANES]
             out[l + 1] = s[:, LANES:]
-        store(c).start()
+            if (i + 2) % STORE == 0:
+                store(c * (CORE_STEP // STORE) + i // STORE).start()
         return 0
 
     lax.fori_loop(0, chunks, project, 0)
@@ -365,7 +367,7 @@
         store(c).wait()
         return 0
 
-    lax.fori_loop(0, chunks, drain, 0)
+    lax.fori_loop(0, x.shape[0] // STORE, drain, 0)
 
 
 def basis_core(x, packed, start, own):
@@ -392,7 +394,7 @@
             pltpu.VMEM((elevs, elevs), jnp.bfloat16),
             pltpu.SemaphoreType.DMA((chunks,)),
             pltpu.SemaphoreType.DMA,
-            pltpu.SemaphoreType.DMA((chunks,)),
+            pltpu.SemaphoreType.DMA((lines // STORE,)),
         ],
         compiler_params=pltpu.CompilerParams(vmem_limit_bytes=48 * 1024 * 1024),
         cost_estimate=pl.CostEstimate(

time: 229 us -> 229 us (level)
  no operation moved by 1% of the time
where the time goes in v3:
time: 229 us
  Pallas kernels  228 us (100%)
    pallas_call x1, Pallas kernels, gather_gram(): pl.pallas_call(gather_gram_kernel, out_shape=(jax.ShapeDtypeStruct((lines...  211 us
    pallas_call x1, Pallas kernels, basis_core(): pl.pallas_call(basis_core_kernel, out_shape=(jax.ShapeDtypeStruct((lines,...  16.4 us

profile of v3, /device:TPU:1, one launch (start us, length us, event | category | flops | bytes accessed | tf_op | source)
XLA Modules:
  0.0 228.5 jit_solution(17879074350092688390)
XLA Ops:
  0.6 0.0 copy-start
  0.6 211.3 %gather_gram.1 = (f32[64,512,128]{2,1,0:T(8,128)}, f32[32,40,128]{2,1,0:T(8,128)S(1)}) custom-call(f32[64,32,2048]{2,1,0:T(8,128)} %frames.1), custom_call_target="tpu_custom_call" | custom-call | flops 4294967296 | bytes 50331648 | tf_op jit(solution)/shard_map/gather_gram/pallas_call | solution.py:170
  211.9 0.0 copy-done
  211.9 16.4 %basis_core.1 = (f32[64,96,128]{2,1,0:T(8,128)}, f32[32,96]{1,0:T(8,128)}) custom-call(f32[64,512,128]{2,1,0:T(8,128)} %get-tuple-element.4.x, f32[1280,128]{1,0:T(8,128)S(1)} %bitcast.2, f32[96,512]{1,0:T(8,128)S(1)} %bitcast.3), custom_call_target="tpu_custom_call" | custom-call | flops 2415919104 | bytes 33554432 | tf_op jit(solution)/shard_map/basis_core/pallas_call | solution.py:377
Async XLA Ops:
  0.6 211.3 %copy-start = (f32[512,96]{0,1:T(8,128)S(1)}, f32[512,96]{0,1:T(8,128)}, u32[]{:S(2)}) copy-start(f32[512,96]{0,1:T(8,128)} %param.3) | copy-start | bytes 589828
